TPU v7x, 32 devices: a whole 2x2x4 slice. The times are simulated.
32 devices in a mesh: blk: 16 (over z, x, core), grp: 2 (over y).
Axes of the slice: x: 2, y: 2, z: 4, core: 2. Of those that a mesh axis runs over, the one named last changes fastest.
Arguments:
- raw: bfloat16 [32, 1024, 2400], P(None, ('blk', 'grp')), may hold values from -1200 to 1200
- partner: int32 [3, 16], replicated, may hold values from 0 to 15, as said below
Outputs:
- cross: bfloat16 [3, 256, 1024, 128], P(None, 'grp', 'blk')
Inputs may be any that keep to these rules, and one draw needn't show every extreme that they name: Each row pairs off the 16 blocks: no block is its own partner, and the partner of a block's partner is the block itself. No two rows are equal.
All inputs are finite; a program needn't handle non-finite values.
Results may differ from a plain program's by a relative error of at most 0.0065.
Values may be sent and summed in bfloat16 or wider, within the bound.
A program may use at most 128 MiB of HBM per device.

v0:
```python
import functools
import math

import jax
import jax.numpy as jnp
from jax import lax
from jax.experimental import pallas as pl
from jax.experimental.pallas import tpu as pltpu
from jax.sharding import PartitionSpec as P

F = 256
first_bin = 8
epsilon = 1e-06
GATHER_BYTES = 40 * 2**20


def dft_table(length, num_bins):
    sample_idx = lax.broadcasted_iota(jnp.int32, (length, num_bins), 0)
    bin_index = lax.broadcasted_iota(jnp.int32, (length, num_bins), 1) + first_bin
    phase_angle = (sample_idx * bin_index % length).astype(jnp.float32) * (2.0 * math.pi / length)
    return jnp.concatenate([jnp.cos(phase_angle), -jnp.sin(phase_angle)], axis=1).astype(
        jnp.bfloat16
    )


def whiten(samples, num_bins):
    seg_count, chan_count, length = samples.shape
    spectrum = jnp.dot(
        samples.reshape(seg_count * chan_count, length),
        dft_table(length, num_bins),
        preferred_element_type=jnp.float32,
    ).reshape(seg_count, chan_count, 2, num_bins)
    bin_power = jnp.mean(jnp.sum(spectrum * spectrum, axis=2), axis=0)
    factor = lax.rsqrt(bin_power + epsilon)
    return (spectrum * factor[None, :, None, :]).astype(jnp.bfloat16)


def cross_kernel(scale, rounds, picks_ref, mine_ref, *refs):
    out_ref = refs[rounds]
    bins, _, width = mine_ref.shape
    half = width // 2
    lane = lax.broadcasted_iota(jnp.int32, (half, width), 1)
    sign = jnp.where(lane < half, scale, -scale).astype(jnp.float32)
    for f in range(bins):
        mine = mine_ref[f]
        for r in range(rounds):
            full = lax.dot_general(
                mine, refs[r][0, f], (((0,), (0,)), ((), ())), preferred_element_type=jnp.float32
            )
            turned = pltpu.roll(full[half:], half, 1)
            out_ref[r, f] = (turned * scale + full[:half] * sign).astype(out_ref.dtype)


def cross(mine, gathered, picks, step):
    bins, seg_count, width = mine.shape
    rounds = picks.shape[0]
    half = width // 2
    other = [
        pl.BlockSpec(
            (1, step, seg_count, width), functools.partial(lambda r, i, p: (p[r], i, 0, 0), r)
        )
        for r in range(rounds)
    ]
    return pl.pallas_call(
        functools.partial(cross_kernel, 1.0 / math.sqrt(seg_count), rounds),
        grid_spec=pltpu.PrefetchScalarGridSpec(
            num_scalar_prefetch=1,
            grid=(bins // step,),
            in_specs=[pl.BlockSpec((step, seg_count, width), lambda i, p: (i, 0, 0))] + other,
            out_specs=pl.BlockSpec((rounds, step, half, width), lambda i, p: (0, i, 0, 0)),
        ),
        out_shape=jax.ShapeDtypeStruct((rounds, bins, half, width), jnp.bfloat16),
        compiler_params=pltpu.CompilerParams(vmem_limit_bytes=32 * 2**20),
    )(picks, mine, *[gathered] * rounds)


def per_device(num_blocks, num_grp, raw, partner):
    white = whiten(raw, F)
    seg_count, chan_count, _, _ = white.shape
    own = F // num_grp
    white = lax.all_to_all(white, "grp", split_axis=3, concat_axis=1, tiled=True)
    spectra = jnp.transpose(white, (3, 0, 2, 1)).reshape(
        own, seg_count, 2 * num_grp * chan_count
    )
    picks = lax.dynamic_index_in_dim(partner, lax.axis_index("blk"), 1, keepdims=False)
    chunks = 1
    while spectra.size * 2 * num_blocks // chunks > GATHER_BYTES:
        chunks *= 2

    def one(part):
        return cross(part, lax.all_gather(part, "blk"), picks, 16)

    if chunks == 1:
        return one(spectra)
    result = lax.map(one, spectra.reshape(chunks, own // chunks, seg_count, -1))
    rounds = partner.shape[0]
    return jnp.moveaxis(result, 0, 1).reshape(rounds, own, *result.shape[3:])


def solution(mesh):
    placed = (P(None, ("blk", "grp"), None), P())
    return jax.shard_map(
        functools.partial(per_device, mesh.shape["blk"], mesh.shape["grp"]),
        mesh=mesh,
        in_specs=placed,
        out_specs=P(None, "grp", "blk", None),
        check_vma=False,
    )
```

profile of v0, /device:TPU:1, one launch (start us, length us, event | category | flops | bytes accessed | tf_op | source)
XLA Modules:
  0.0 216.4 jit_solution(2421250597222672216)
XLA Ops:
  6.5 0.0 copy-start
  6.5 0.0 all-gather.2.cloned.1.call-start
  6.5 10.4 %cosine_convert_fusion = (bf16[2400,256]{1,0:T(8,128)(2,1)S(1)}, bf16[2400,256]{1,0:T(8,128)(2,1)S(1)}) fusion(s32[256]{0:T(256)S(1)} %iota_add_fusion), kind=kLoop, calls=%fused_computation.8 | loop fusion | flops 7372800 | bytes 2458624 | tf_op jit(solution)/shard_map/convert
  16.9 4.9 %fusion.9 = f32[1024,512]{0,1:T(8,128)S(1)} fusion(bf16[1024,2400]{1,0:T(8,128)(2,1)} %bitcast.20, bf16[2400,256]{1,0:T(8,128)(2,1)S(1)} %get-tuple-element.6, bf16[2400,256]{1,0:T(8,128)(2,1)S(1)} %get-tuple-element.5), kind=kOutput, calls=%fused_computation.15 | convolution fusion | flops 2521497600 | bytes 9469952 | tf_op jit(solution)/shard_map/dot_general | solution.py:28
  21.8 1.8 copy.18
  23.6 2.6 %reshape.15 = f32[32,32,2,256]{3,2,1,0:T(2,128)S(1)} reshape(f32[1024,512]{1,0:T(8,128)} %copy.18) | data formatting | bytes 4194304 | tf_op jit(solution)/shard_map/reshape | solution.py:32
  26.2 0.9 multiply_reduce_fusion
  27.2 0.9 multiply_convert_fusion
  28.1 5.7 %copy.19 = bf16[32,32,2,256]{1,0,2,3:T(8,128)(2,1)} copy(bf16[32,32,2,256]{3,2,1,0:T(2,128)(2,1)S(1)} %multiply_convert_fusion) | data formatting | bytes 2097152 | tf_op jit(solution)/shard_map/convert_element_type | solution.py:35
  33.8 5.7 %reshape.18 = bf16[2,2,131072]{2,1,0:T(2,128)(2,1)S(1)} reshape(bf16[256,2,32,32]{3,2,1,0:T(8,128)(2,1)} %bitcast.15) | data formatting | bytes 2097152
  39.5 15.8 %all_to_all.18 = bf16[2,2,131072]{2,1,0:T(2,128)(2,1)S(1)} all-to-all(bf16[2,2,131072]{2,1,0:T(2,128)(2,1)S(1)} %reshape.18), channel_id=1, replica_groups=mesh['blk'=16,'grp'=2] {'grp'}, dimensions={0} | all-to-all | bytes 2097152 | tf_op jit(solution)/shard_map/all_to_all | solution.py:81
  55.3 3.3 %reshape.19 = bf16[256,2,32,32]{3,2,1,0:T(8,128)(2,1)} reshape(bf16[2,2,131072]{2,1,0:T(2,128)(2,1)S(1)} %all_to_all.18) | data formatting | bytes 2097152
  58.6 6.3 %copy.24 = bf16[32,32,2,2,128]{4,3,1,2,0:T(2,128)(2,1)S(1)} copy(bf16[32,32,2,2,128]{1,0,2,4,3:T(8,128)(2,1)} %bitcast.16) | data formatting | bytes 2097152 | tf_op jit(solution)/shard_map/all_to_all | solution.py:81
  64.9 0.3 copy.21
  65.2 1.7 copy.22
  66.9 0.0 all-gather.2.cloned.1.call-update
  66.9 0.0 copy-done
  66.9 0.2 dynamic-slice_reduce_fusion.picks_ref
  67.1 1.0 copy.23.mine_ref
  68.1 127.9 %all-gather.2.cloned.1.call-done.refs_0_.refs_1_.refs_2_ = bf16[16,128,32,128]{3,2,1,0:T(8,128)(2,1)} async-done(((bf16[1,128,32,128]{3,2,1,0:T(8,128)(2,1)}), bf16[16,128,32,128]{3,2,1,0:T(8,128)(2,1)}) %all-gather.2.cloned.1.call-update) | async-done | bytes 16777232 | tf_op jit(solution)/shard_map/all_gather | solution.py:91
  196.0 0.0 copy-start.1
  196.0 5.8 %copy-done.1 = bf16[16,128,32,128]{3,2,1,0:T(8,128)(2,1)S(1)} copy-done((bf16[16,128,32,128]{3,2,1,0:T(8,128)(2,1)S(1)}, bf16[16,128,32,128]{3,2,1,0:T(8,128)(2,1)}, u32[]{:S(2)}) %copy-start.1) | copy-done | bytes 16777240
  201.8 7.8 %shard_map.28 = bf16[3,128,64,128]{3,2,1,0:T(8,128)(2,1)} custom-call(s32[3]{0:T(128)S(1)} %dynamic-slice_reduce_fusion.picks_ref, bf16[128,32,128]{2,1,0:T(8,128)(2,1)S(1)} %copy.23.mine_ref, bf16[16,128,32,128]{3,2,1,0:T(8,128)(2,1)S(1)} %copy-done.1, bf16[16,128,32,128]{3,2,1,0:T(8,128)(2,1)S(1)} %copy-done.1, bf16[16,128,32,128]{3,2,1,0:T(8,128)(2,1)S(1)} %copy-done.1), custom_call_target="tpu_custom_call" | custom-call | tf_op jit(solution)/shard_map/pallas_call | solution.py:64
  (2 shorter events, 0.0 us)
Async XLA Ops:
  6.5 60.4 %copy-start = (s32[3,16]{1,0:T(4,128)S(1)}, s32[3,16]{1,0:T(4,128)}, u32[]{:S(2)}) copy-start(s32[3,16]{1,0:T(4,128)} %param.3) | copy-start | bytes 580
  6.5 189.5 %all-gather.2.cloned.1.call-start = ((), (), s32[]{:S(2)}) async-start(), calls=%async_computation.1 | async-start | bytes 17825792 | tf_op jit(solution)/shard_map/all_gather | solution.py:91
  196.0 5.8 %copy-start.1 = (bf16[16,128,32,128]{3,2,1,0:T(8,128)(2,1)S(1)}, bf16[16,128,32,128]{3,2,1,0:T(8,128)(2,1)}, u32[]{:S(2)}) copy-start(bf16[16,128,32,128]{3,2,1,0:T(8,128)(2,1)} %all-gather.2.cloned.1.call-done.refs_0_.refs_1_.refs_2_) | copy-start | bytes 50331652
Sparse Core Ops, SparseCore 0:
  67.0 128.9 all-gather.1
where the time goes:
time: 217 us; the launch traced here: 216 us
  waiting for transfers between devices  128 us (59%)
  local copies, waits for them, and re-layouts  34.2 us (16%)
  blocking collectives  15.8 us (7%)
  between operations  13.5 us (6%)
  other arithmetic  12.3 us (6%)
  Pallas kernels  7.76 us (4%)
  matrix products  4.9 us (2%)
    all_gather x1, waiting for transfers between devices, one(): return cross(part, lax.all_gather(part, 'blk'), picks, 16)  128 us
    all_to_all x1, blocking collectives, per_device(): lax.all_to_all(white, 'grp', split_axis=3, concat_axis=1, tiled=True)  15.8 us
    unnamed x6, local copies, waits for them, and re-layouts  14.7 us
    another operation x1, other arithmetic  10.4 us
    pallas_call x1, Pallas kernels, cross(): pl.pallas_call(functools.partial(cross_kernel, 1.0 / math.sqrt(seg_count)...  7.76 us
    all_to_all x2, local copies, waits for them, and re-layouts, per_device(): lax.all_to_all(white, 'grp', split_axis=3, concat_axis=1, tiled=True)  6.6 us
    convert_element_type x1, local copies, waits for them, and re-layouts, whiten(): return (spectrum * factor[None, :, None, :]).astype(jnp.bfloat16)  5.69 us
    dot_general x1, matrix products, whiten(): jnp.dot(samples.reshape(seg_count * chan_count, length), dft_table(length...  4.9 us
  transfers between devices with their start and end apart: 1, of which 1 were waited for; matrix products, arithmetic and copies ran while one was open for 1% of the time, Pallas kernels for 0%

commit v1 on v0

--- a/solution.py
+++ b/solution.py
@@ -14,13 +14,23 @@
 GATHER_BYTES = 40 * 2**20
 
 
+COARSE = 32
+
+
 def dft_table(length, num_bins):
-    sample_idx = lax.broadcasted_iota(jnp.int32, (length, num_bins), 0)
-    bin_index = lax.broadcasted_iota(jnp.int32, (length, num_bins), 1) + first_bin
-    phase_angle = (sample_idx * bin_index % length).astype(jnp.float32) * (2.0 * math.pi / length)
-    return jnp.concatenate([jnp.cos(phase_angle), -jnp.sin(phase_angle)], axis=1).astype(
-        jnp.bfloat16
+    bins = lax.broadcasted_iota(jnp.int32, (1, num_bins), 1) + first_bin
+    unit = 2.0 * math.pi / length
+
+    def pair(times):
+        phase = (times[:, None] * bins % length).astype(jnp.float32) * unit
+        return jnp.cos(phase), jnp.sin(phase)
+
+    cos_a, sin_a = (t[:, None, :] for t in pair(jnp.arange(length // COARSE, dtype=jnp.int32) * COARSE))
+    cos_b, sin_b = (t[None] for t in pair(jnp.arange(COARSE, dtype=jnp.int32)))
+    table = jnp.concatenate(
+        [cos_a * cos_b - sin_a * sin_b, -(sin_a * cos_b + cos_a * sin_b)], axis=2
     )
+    return table.reshape(length, 2 * num_bins).astype(jnp.bfloat16)
 
 
 def whiten(samples, num_bins):
@@ -29,10 +39,12 @@
         samples.reshape(seg_count * chan_count, length),
         dft_table(length, num_bins),
         preferred_element_type=jnp.float32,
-    ).reshape(seg_count, chan_count, 2, num_bins)
-    bin_power = jnp.mean(jnp.sum(spectrum * spectrum, axis=2), axis=0)
+    ).reshape(seg_count, chan_count, 2 * num_bins)
+    real_part = spectrum[:, :, :num_bins]
+    imag_part = spectrum[:, :, num_bins:]
+    bin_power = jnp.mean(real_part * real_part + imag_part * imag_part, axis=0)
     factor = lax.rsqrt(bin_power + epsilon)
-    return (spectrum * factor[None, :, None, :]).astype(jnp.bfloat16)
+    return jnp.stack([real_part * factor, imag_part * factor], axis=0).astype(jnp.bfloat16)
 
 
 def cross_kernel(scale, rounds, picks_ref, mine_ref, *refs):
@@ -70,16 +82,127 @@
             out_specs=pl.BlockSpec((rounds, step, half, width), lambda i, p: (0, i, 0, 0)),
         ),
         out_shape=jax.ShapeDtypeStruct((rounds, bins, half, width), jnp.bfloat16),
-        compiler_params=pltpu.CompilerParams(vmem_limit_bytes=32 * 2**20),
+        compiler_params=pltpu.CompilerParams(vmem_limit_bytes=56 * 2**20),
     )(picks, mine, *[gathered] * rounds)
+
+
+def gather_kernel(outer, cuts, x_ref, out_ref, z_sem, x_sem, c_sem, recv_sem):
+    me = lax.axis_index("blk")
+    o, m, c = me // 4, me // 2 % 2, me % 2
+    pieces = len(cuts) - 1
+
+    def index(o_, m_, c_):
+        return (o_ * 2 + m_) * 2 + c_
+
+    left, right = index(o - 1, m, c), index(o + 1, m, c)
+    across, sibling = index(o, 1 - m, c), index(o, m, 1 - c)
+    has_left, has_right = o > 0, o < outer - 1
+
+    def copy(block, q, target, sem, own=False):
+        part = pl.ds(cuts[q], cuts[q + 1] - cuts[q])
+        there = out_ref.at[block, part]
+        return pltpu.make_async_remote_copy(
+            src_ref=x_ref.at[part] if own else there,
+            dst_ref=there,
+            send_sem=sem,
+            recv_sem=recv_sem.at[block, q],
+            device_id={"blk": target},
+            device_id_type=pl.DeviceIdType.MESH,
+        )
+
+    def forward(act, o_, side, q, to_left, to_right, own=False):
+        block = index(o_, m if side == 0 else 1 - m, c)
+        if to_left:
+            pl.when(has_left)(lambda: act(copy(block, q, left, z_sem.at[0, side, o_, q], own)))
+        if to_right:
+            pl.when(has_right)(lambda: act(copy(block, q, right, z_sem.at[1, side, o_, q], own)))
+        if side == 0 and (own or q > 0):
+            act(copy(block, q, across, x_sem.at[o_, q], own))
+        act(copy(block, q, sibling, c_sem.at[side, o_, q], own))
+
+    def sweep(act, arrive):
+        for q in range(pieces):
+            forward(act, o, 0, q, True, True, own=True)
+        for step in range(1, outer + 1):
+            for q in range(pieces):
+                for side, far in ((0, step), (1, step - 1)):
+                    line = side == 0 or q == 0
+                    if far == 0:
+                        arrive(o, side, q)
+                        forward(act, o, side, q, line, line)
+                    elif far < outer:
+
+                        @pl.when(o - far >= 0)
+                        def _():
+                            arrive(o - far, side, q)
+                            forward(act, o - far, side, q, False, line)
+
+                        @pl.when(o + far < outer)
+                        def _():
+                            arrive(o + far, side, q)
+                            forward(act, o + far, side, q, line, False)
+
+    def arrive(o_, side, q):
+        copy(index(o_, m if side == 0 else 1 - m, c), q, sibling, c_sem.at[0, 0, 0]).wait_recv()
+
+    barrier = pltpu.get_barrier_semaphore()
+
+    def greet(target):
+        pl.semaphore_signal(
+            barrier, inc=1, device_id={"blk": target}, device_id_type=pl.DeviceIdType.MESH
+        )
+
+    greet(across)
+    greet(sibling)
+    pl.when(has_left)(lambda: greet(left))
+    pl.when(has_right)(lambda: greet(right))
+    pl.semaphore_wait(barrier, 2 + jnp.minimum(o, 1) + jnp.minimum(outer - 1 - o, 1))
+
+    sweep(lambda d: d.start(), arrive)
+    for o_ in range(outer):
+        for m_ in range(2):
+            for q in range(pieces):
+                copy(index(o_, m_, 1 - c), q, sibling, c_sem.at[0, 0, 0]).wait_recv()
+    sweep(lambda d: d.wait_send(), lambda *_: None)
+
+
+def gather(block, num_blocks):
+    bins = block.shape[0]
+    outer = num_blocks // 4
+    cuts = tuple(bins * k // 16 for k in (0, 3, 7, 11, 16))
+    pieces = len(cuts) - 1
+    return pl.pallas_call(
+        functools.partial(gather_kernel, outer, cuts),
+        out_shape=jax.ShapeDtypeStruct((num_blocks, *block.shape), block.dtype),
+        in_specs=[pl.BlockSpec(memory_space=pl.ANY)],
+        out_specs=pl.BlockSpec(memory_space=pl.ANY),
+        scratch_shapes=[
+            pltpu.SemaphoreType.DMA((2, 2, outer, pieces)),
+            pltpu.SemaphoreType.DMA((outer, pieces)),
+            pltpu.SemaphoreType.DMA((2, outer, pieces)),
+            pltpu.SemaphoreType.DMA((num_blocks, pieces)),
+        ],
+        compiler_params=pltpu.CompilerParams(
+            collective_id=0, has_side_effects=True, vmem_limit_bytes=56 * 2**20
+        ),
+    )(block)
 
 
 def per_device(num_blocks, num_grp, raw, partner):
     white = whiten(raw, F)
-    seg_count, chan_count, _, _ = white.shape
+    _, seg_count, chan_count, _ = white.shape
     own = F // num_grp
-    white = lax.all_to_all(white, "grp", split_axis=3, concat_axis=1, tiled=True)
-    spectra = jnp.transpose(white, (3, 0, 2, 1)).reshape(
+    if num_grp == 2:
+        me = lax.axis_index("grp")
+        kept = lax.dynamic_slice_in_dim(white, me * own, own, 3)
+        sent = lax.dynamic_slice_in_dim(white, (1 - me) * own, own, 3)
+        got = lax.ppermute(sent, "grp", [(0, 1), (1, 0)])
+        white = jnp.concatenate(
+            [jnp.where(me == 0, kept, got), jnp.where(me == 0, got, kept)], axis=2
+        )
+    else:
+        white = lax.all_to_all(white, "grp", split_axis=3, concat_axis=2, tiled=True)
+    spectra = jnp.transpose(white, (3, 1, 0, 2)).reshape(
         own, seg_count, 2 * num_grp * chan_count
     )
     picks = lax.dynamic_index_in_dim(partner, lax.axis_index("blk"), 1, keepdims=False)
@@ -87,8 +210,11 @@
     while spectra.size * 2 * num_blocks // chunks > GATHER_BYTES:
         chunks *= 2
 
+    direct = chunks == 1 and num_blocks % 4 == 0
+
     def one(part):
-        return cross(part, lax.all_gather(part, "blk"), picks, 16)
+        whole = gather(part, num_blocks) if direct else lax.all_gather(part, "blk")
+        return cross(part, whole, picks, 16)
 
     if chunks == 1:
         return one(spectra)

time: 217 us -> 130 us (0.60)
  waiting for transfers between devices: 128 us -> 10.9 us
  Pallas kernels: 7.76 us -> 103 us
  local copies, waits for them, and re-layouts: 34.2 us -> 4.48 us
  blocking collectives: 15.8 us -> 0 us
  between operations: 13.5 us -> 0.09 us
  other arithmetic: 12.3 us -> 2.21 us
    all_gather x1 -> x0, waiting for transfers between devices: 128 us -> none  [one(): return cross(part, lax.all_gather(part, 'blk'), picks, 16)]
    pallas_call x0 -> x1, Pallas kernels: none -> 92.4 us  [gather(): pl.pallas_call(functools.partial(gather_kernel, outer, cuts), out_shape=j...]
    all_to_all x1 -> x0, blocking collectives: 15.8 us -> none  [per_device(): lax.all_to_all(white, 'grp', split_axis=3, concat_axis=1, tiled=True)]
    unnamed x6 -> x2, local copies, waits for them, and re-layouts: 14.7 us -> 0.01 us
    ppermute x0 -> x1, waiting for transfers between devices: none -> 10.9 us  [per_device(): got = lax.ppermute(sent, 'grp', [(0, 1), (1, 0)])]
    another operation x1 -> x3, other arithmetic: 10.4 us -> 1.12 us
    all_to_all x2 -> x0, local copies, waits for them, and re-layouts: 6.6 us -> none  [per_device(): lax.all_to_all(white, 'grp', split_axis=3, concat_axis=1, tiled=True)]
    convert_element_type x1 -> x0, local copies, waits for them, and re-layouts: 5.69 us -> none  [whiten(): return (spectrum * factor[None, :, None, :]).astype(jnp.bfloat16)]
where the time goes in v1:
time: 130 us; the launch traced here: 129 us
  Pallas kernels  103 us (79%)
  waiting for transfers between devices  10.9 us (8%)
  matrix products  6.68 us (5%)
  local copies, waits for them, and re-layouts  4.48 us (3%)
  other arithmetic  2.21 us (2%)
  starting transfers between devices  2.14 us (2%)
    pallas_call x1, Pallas kernels, gather(): pl.pallas_call(functools.partial(gather_kernel, outer, cuts), out_shape=j...  92.4 us
    ppermute x1, waiting for transfers between devices, per_device(): got = lax.ppermute(sent, 'grp', [(0, 1), (1, 0)])  10.9 us
    pallas_call x1, Pallas kernels, cross(): pl.pallas_call(functools.partial(cross_kernel, 1.0 / math.sqrt(seg_count)...  10.6 us
    dot_general x1, matrix products, whiten(): jnp.dot(samples.reshape(seg_count * chan_count, length), dft_table(length...  6.68 us
  transfers between devices with their start and end apart: 1, of which 1 were waited for; matrix products, arithmetic and copies ran while one was open for 1% of the time, Pallas kernels for 0%

profile of v1, /device:TPU:1, one launch (start us, length us, event | category | flops | bytes accessed | tf_op | source)
XLA Modules:
  0.0 129.4 jit_solution(18034622894532961873)
XLA Ops:
  0.0 0.0 copy-start
  0.0 0.2 fusion.23
  0.2 0.4 fusion.16
  0.6 0.7 subtract_convert_fusion
  1.3 6.7 %fusion.4 = f32[1024,512]{0,1:T(8,128)} fusion(bf16[1024,2400]{1,0:T(8,128)(2,1)} %bitcast.19, bf16[2400,256]{1,0:T(8,128)(2,1)S(1)} %bitcast.18, bf16[2400,256]{1,0:T(8,128)(2,1)S(1)} %bitcast.17), kind=kOutput, calls=%fused_computation.6 | convolution fusion | flops 2521497600 | bytes 9469952 | tf_op jit(solution)/shard_map/dot_general | solution.py:38
  8.0 1.9 %copy.4 = f32[1024,512]{1,0:T(8,128)S(1)} copy(f32[1024,512]{0,1:T(8,128)} %fusion.4) | data formatting | bytes 4194304 | tf_op jit(solution)/shard_map/dot_general | solution.py:38
  9.9 0.1 add_reduce_fusion
  10.1 0.3 fusion.8
  10.4 0.1 fusion.9
  10.5 2.1 %collective-permute-start = (bf16[2,32,32,128]{3,2,1,0:T(8,128)(2,1)S(1)}, bf16[2,32,32,128]{3,2,1,0:T(8,128)(2,1)S(1)}, u32[]{:S(2)}, u32[]{:S(2)}) collective-permute-start(bf16[2,32,32,128]{3,2,1,0:T(8,128)(2,1)S(1)} %fusion.9), channel_id=1, source_target_pairs={{0,1},{1,0},{2,3},{3,2},{4,5},{5,4},{6,7},{7,6},{8,9},{9,8},{10,11... | collective-permute-start | bytes 1572872 | tf_op jit(solution)/shard_map/ppermute | solution.py:199
  12.7 0.0 copy-done
  12.7 0.8 dynamic-slice_reduce_fusion.picks_ref
  13.4 10.9 %collective-permute-done = bf16[2,32,32,128]{3,2,1,0:T(8,128)(2,1)S(1)} collective-permute-done((bf16[2,32,32,128]{3,2,1,0:T(8,128)(2,1)S(1)}, bf16[2,32,32,128]{3,2,1,0:T(8,128)(2,1)S(1)}, u32[]{:S(2)}, u32[]{:S(2)}) %collective-permute-start) | collective-permute-done | bytes 524320 | tf_op jit(solution)/shard_map/ppermute | solution.py:199
  24.3 0.2 broadcast_select_fusion.1
  24.5 0.1 maximum_bitcast_fusion
  24.7 0.1 copy.5
  24.8 1.7 %copy.7.x_ref.mine_ref = bf16[128,32,128]{2,1,0:T(8,128)(2,1)} copy(bf16[128,32,128]{0,2,1:T(8,128)(2,1)S(1)} %bitcast.16) | data formatting | bytes 2097152 | tf_op jit(solution)/shard_map/reshape | solution.py:205
  26.5 92.4 %shard_map.28.refs_0_.refs_1_.refs_2_ = bf16[16,128,32,128]{3,2,1,0:T(8,128)(2,1)} custom-call(bf16[128,32,128]{2,1,0:T(8,128)(2,1)} %copy.7.x_ref.mine_ref), custom_call_target="tpu_custom_call" | custom-call | tf_op jit(solution)/shard_map/pallas_call | solution.py:174
  118.9 10.6 %shard_map.29 = bf16[3,128,64,128]{3,2,1,0:T(8,128)(2,1)} custom-call(s32[3]{0:T(128)} %dynamic-slice_reduce_fusion.picks_ref, bf16[128,32,128]{2,1,0:T(8,128)(2,1)} %copy.7.x_ref.mine_ref, bf16[16,128,32,128]{3,2,1,0:T(8,128)(2,1)} %shard_map.28.refs_0_.refs_1_.refs_2_, bf16[16,128,32,128]{3,2,1,0:T(8,128)(2,1)} %shard_map.28.refs_0_.refs_1_.refs_2_, ...), custom_call_target="tpu_custom_call" | custom-call | tf_op jit(solution)/shard_map/pallas_call | solution.py:76
  (3 shorter events, 0.0 us)
Async XLA Ops:
  0.0 12.7 %copy-start = (s32[3,16]{1,0:T(4,128)S(1)}, s32[3,16]{1,0:T(4,128)}, u32[]{:S(2)}) copy-start(s32[3,16]{1,0:T(4,128)} %param.3) | copy-start | bytes 580
  10.5 13.8 %collective-permute-start = (bf16[2,32,32,128]{3,2,1,0:T(8,128)(2,1)S(1)}, bf16[2,32,32,128]{3,2,1,0:T(8,128)(2,1)S(1)}, u32[]{:S(2)}, u32[]{:S(2)}) collective-permute-start(bf16[2,32,32,128]{3,2,1,0:T(8,128)(2,1)S(1)} %fusion.9), channel_id=1, source_target_pairs={{0,1},{1,0},{2,3},{3,2},{4,5},{5,4},{6,7},{7,6},{8,9},{9,8},{10,11... | collective-permute-start | bytes 1572872 | tf_op jit(solution)/shard_map/ppermute | solution.py:199

commit v2 on v1

--- a/solution.py
+++ b/solution.py
@@ -17,8 +17,8 @@
 COARSE = 32
 
 
-def dft_table(length, num_bins):
-    bins = lax.broadcasted_iota(jnp.int32, (1, num_bins), 1) + first_bin
+def dft_table(length, first, num_bins):
+    bins = lax.broadcasted_iota(jnp.int32, (1, num_bins), 1) + first
     unit = 2.0 * math.pi / length
 
     def pair(times):
@@ -33,11 +33,11 @@
     return table.reshape(length, 2 * num_bins).astype(jnp.bfloat16)
 
 
-def whiten(samples, num_bins):
+def whiten(samples, first, num_bins):
     seg_count, chan_count, length = samples.shape
     spectrum = jnp.dot(
         samples.reshape(seg_count * chan_count, length),
-        dft_table(length, num_bins),
+        dft_table(length, first, num_bins),
         preferred_element_type=jnp.float32,
     ).reshape(seg_count, chan_count, 2 * num_bins)
     real_part = spectrum[:, :, :num_bins]
@@ -169,7 +169,7 @@
 def gather(block, num_blocks):
     bins = block.shape[0]
     outer = num_blocks // 4
-    cuts = tuple(bins * k // 16 for k in (0, 3, 7, 11, 16))
+    cuts = tuple(bins * k // 16 for k in (0, 2, 7, 12, 16))
     pieces = len(cuts) - 1
     return pl.pallas_call(
         functools.partial(gather_kernel, outer, cuts),
@@ -189,19 +189,17 @@
 
 
 def per_device(num_blocks, num_grp, raw, partner):
-    white = whiten(raw, F)
-    _, seg_count, chan_count, _ = white.shape
+    seg_count, chan_count, _ = raw.shape
     own = F // num_grp
     if num_grp == 2:
         me = lax.axis_index("grp")
-        kept = lax.dynamic_slice_in_dim(white, me * own, own, 3)
-        sent = lax.dynamic_slice_in_dim(white, (1 - me) * own, own, 3)
-        got = lax.ppermute(sent, "grp", [(0, 1), (1, 0)])
+        got = lax.ppermute(whiten(raw, first_bin + (1 - me) * own, own), "grp", [(0, 1), (1, 0)])
+        kept = whiten(raw, first_bin + me * own, own)
         white = jnp.concatenate(
             [jnp.where(me == 0, kept, got), jnp.where(me == 0, got, kept)], axis=2
         )
     else:
-        white = lax.all_to_all(white, "grp", split_axis=3, concat_axis=2, tiled=True)
+        white = lax.all_to_all(whiten(raw, first_bin, F), "grp", split_axis=3, concat_axis=2, tiled=True)
     spectra = jnp.transpose(white, (3, 1, 0, 2)).reshape(
         own, seg_count, 2 * num_grp * chan_count
     )

time: 130 us -> 124 us (0.954)
  waiting for transfers between devices: 10.9 us -> 6.6 us
  Pallas kernels: 103 us -> 100 us
  other arithmetic: 2.21 us -> 3.86 us
  matrix products: 6.68 us -> 8.05 us
    ppermute x1, waiting for transfers between devices: 10.9 us -> 6.6 us  [per_device(): lax.ppermute(whiten(raw, first_bin + (1 - me) * own, own), 'grp', [(0, 1)...]
    pallas_call x1, Pallas kernels: 92.4 us -> 89.5 us  [gather(): pl.pallas_call(functools.partial(gather_kernel, outer, cuts), out_shape=j...]
    dot_general x1 -> x2, matrix products: 6.68 us -> 8.05 us  [whiten(): jnp.dot(samples.reshape(seg_count * chan_count, length), dft_table(length...]
  transfers between devices with their start and end apart: 1 -> 1, of which waited for: 1 -> 1; matrix products, arithmetic and copies ran while one was open for 1% -> 4% of each run, Pallas kernels for 0% -> 0%
where the time goes in v2:
time: 124 us
  Pallas kernels  100 us (81%)
  matrix products  8.05 us (6%)
  waiting for transfers between devices  6.6 us (5%)
  other arithmetic  3.86 us (3%)
  local copies, waits for them, and re-layouts  3.24 us (3%)
  starting transfers between devices  2.07 us (2%)
    pallas_call x1, Pallas kernels, gather(): pl.pallas_call(functools.partial(gather_kernel, outer, cuts), out_shape=j...  89.5 us
    pallas_call x1, Pallas kernels, cross(): pl.pallas_call(functools.partial(cross_kernel, 1.0 / math.sqrt(seg_count)...  10.6 us
    dot_general x2, matrix products, whiten(): jnp.dot(samples.reshape(seg_count * chan_count, length), dft_table(length...  8.05 us
    ppermute x1, waiting for transfers between devices, per_device(): lax.ppermute(whiten(raw, first_bin + (1 - me) * own, own), 'grp', [(0, 1)...  6.6 us
  transfers between devices with their start and end apart: 1, of which 1 were waited for; matrix products, arithmetic and copies ran while one was open for 4% of the time, Pallas kernels for 0%

profile of v2, /device:TPU:1, one launch (start us, length us, event | category | flops | bytes accessed | tf_op | source)
XLA Modules:
  0.0 124.0 jit_solution(17693095331615434141)
XLA Ops:
  0.0 0.0 copy-start
  0.0 0.1 fusion.31
  0.1 0.1 fusion.35
  0.2 0.4 fusion.21
  0.6 0.7 subtract_convert_fusion
  1.4 4.0 %convolution_bitcast_fusion = f32[1024,256]{0,1:T(8,128)S(1)} fusion(bf16[1024,2400]{1,0:T(8,128)(2,1)} %bitcast.33, bf16[2400,128]{1,0:T(8,128)(2,1)S(1)} %bitcast.32, bf16[2400,128]{1,0:T(8,128)(2,1)S(1)} %bitcast.31), kind=kOutput, calls=%fused_computation | convolution fusion | flops 1260748800 | bytes 7192576 | tf_op jit(solution)/shard_map/dot_general | solution.py:38
  5.4 0.3 copy.6
  5.7 0.1 add_reduce_fusion
  5.8 0.1 fusion.8
  5.9 0.8 pad_maximum_fusion.1
  6.8 2.1 %collective-permute-start = (bf16[2,32,32,128]{3,2,1,0:T(8,128)(2,1)}, bf16[2,32,32,128]{3,2,1,0:T(8,128)(2,1)}, u32[]{:S(2)}, u32[]{:S(2)}) collective-permute-start(bf16[2,32,32,128]{3,2,1,0:T(8,128)(2,1)} %pad_maximum_fusion.1), channel_id=1, source_target_pairs={{0,1},{1,0},{2,3},{3,2},{4,5},{5,4},{6,7},{7,6},{8,9},{9,8},{10,11... | collective-permute-start | bytes 1572872 | tf_op jit(solution)/shard_map/ppermute | solution.py:196
  8.8 4.0 %convolution_bitcast_fusion.1 = f32[1024,256]{0,1:T(8,128)S(1)} fusion(bf16[1024,2400]{1,0:T(8,128)(2,1)} %bitcast.34, bf16[2400,128]{1,0:T(8,128)(2,1)S(1)} %bitcast.29, bf16[2400,128]{1,0:T(8,128)(2,1)S(1)} %bitcast.30), kind=kOutput, calls=%fused_computation.1 | convolution fusion | flops 1260748800 | bytes 7192576 | tf_op jit(solution)/shard_map/dot_general | solution.py:38
  12.9 0.3 copy.5
  13.2 0.1 add_reduce_fusion.1
  13.3 0.0 copy-done
  13.3 0.8 dynamic-slice_reduce_fusion.picks_ref
  14.1 0.1 fusion.6
  14.2 6.6 %collective-permute-done = bf16[2,32,32,128]{3,2,1,0:T(8,128)(2,1)} collective-permute-done((bf16[2,32,32,128]{3,2,1,0:T(8,128)(2,1)}, bf16[2,32,32,128]{3,2,1,0:T(8,128)(2,1)}, u32[]{:S(2)}, u32[]{:S(2)}) %collective-permute-start) | collective-permute-done | bytes 524320 | tf_op jit(solution)/shard_map/ppermute | solution.py:196
  20.8 1.2 broadcast_select_fusion.1
  22.0 0.1 maximum_bitcast_fusion
  22.1 0.1 copy.7
  22.2 1.7 %copy.9.x_ref.mine_ref = bf16[128,32,128]{2,1,0:T(8,128)(2,1)} copy(bf16[128,32,128]{0,2,1:T(8,128)(2,1)S(1)} %bitcast.28) | data formatting | bytes 2097152 | tf_op jit(solution)/shard_map/reshape | solution.py:203
  23.9 89.5 %shard_map.28.refs_0_.refs_1_.refs_2_ = bf16[16,128,32,128]{3,2,1,0:T(8,128)(2,1)} custom-call(bf16[128,32,128]{2,1,0:T(8,128)(2,1)} %copy.9.x_ref.mine_ref), custom_call_target="tpu_custom_call" | custom-call | tf_op jit(solution)/shard_map/pallas_call | solution.py:174
  113.4 10.6 %shard_map.29 = bf16[3,128,64,128]{3,2,1,0:T(8,128)(2,1)} custom-call(s32[3]{0:T(128)} %dynamic-slice_reduce_fusion.picks_ref, bf16[128,32,128]{2,1,0:T(8,128)(2,1)} %copy.9.x_ref.mine_ref, bf16[16,128,32,128]{3,2,1,0:T(8,128)(2,1)} %shard_map.28.refs_0_.refs_1_.refs_2_, bf16[16,128,32,128]{3,2,1,0:T(8,128)(2,1)} %shard_map.28.refs_0_.refs_1_.refs_2_, ...), custom_call_target="tpu_custom_call" | custom-call | tf_op jit(solution)/shard_map/pallas_call | solution.py:76
  (5 shorter events, 0.0 us)
Async XLA Ops:
  0.0 13.3 %copy-start = (s32[3,16]{1,0:T(4,128)S(1)}, s32[3,16]{1,0:T(4,128)}, u32[]{:S(2)}) copy-start(s32[3,16]{1,0:T(4,128)} %param.3) | copy-start | bytes 580
  6.8 14.0 %collective-permute-start = (bf16[2,32,32,128]{3,2,1,0:T(8,128)(2,1)}, bf16[2,32,32,128]{3,2,1,0:T(8,128)(2,1)}, u32[]{:S(2)}, u32[]{:S(2)}) collective-permute-start(bf16[2,32,32,128]{3,2,1,0:T(8,128)(2,1)} %pad_maximum_fusion.1), channel_id=1, source_target_pairs={{0,1},{1,0},{2,3},{3,2},{4,5},{5,4},{6,7},{7,6},{8,9},{9,8},{10,11... | collective-permute-start | bytes 1572872 | tf_op jit(solution)/shard_map/ppermute | solution.py:196

commit v3 on v2

--- a/solution.py
+++ b/solution.py
@@ -169,7 +169,7 @@
 def gather(block, num_blocks):
     bins = block.shape[0]
     outer = num_blocks // 4
-    cuts = tuple(bins * k // 16 for k in (0, 2, 7, 12, 16))
+    cuts = tuple(bins * k // 16 for k in (0, 2, 5, 8, 11, 14, 16))
     pieces = len(cuts) - 1
     return pl.pallas_call(
         functools.partial(gather_kernel, outer, cuts),

time: 124 us -> 125 us (level)
  no operation moved by 1% of the time
where the time goes in v3:
time: 125 us; the launch traced here: 124 us
  Pallas kernels  100 us (80%)
  matrix products  8.05 us (6%)
  waiting for transfers between devices  6.6 us (5%)
  other arithmetic  3.86 us (3%)
  local copies, waits for them, and re-layouts  3.24 us (3%)
  starting transfers between devices  2.07 us (2%)
    pallas_call x1, Pallas kernels, gather(): pl.pallas_call(functools.partial(gather_kernel, outer, cuts), out_shape=j...  89.8 us
    pallas_call x1, Pallas kernels, cross(): pl.pallas_call(functools.partial(cross_kernel, 1.0 / math.sqrt(seg_count)...  10.6 us
    dot_general x2, matrix products, whiten(): jnp.dot(samples.reshape(seg_count * chan_count, length), dft_table(length...  8.05 us
    ppermute x1, waiting for transfers between devices, per_device(): lax.ppermute(whiten(raw, first_bin + (1 - me) * own, own), 'grp', [(0, 1)...  6.6 us
  transfers between devices with their start and end apart: 1, of which 1 were waited for; matrix products, arithmetic and copies ran while one was open for 4% of the time, Pallas kernels for 0%

profile of v3, /device:TPU:1, one launch (start us, length us, event | category | flops | bytes accessed | tf_op | source)
XLA Modules:
  0.0 124.4 jit_solution(5399317406878277581)
XLA Ops:
  0.0 0.0 copy-start
  0.0 0.1 fusion.31
  0.1 0.1 fusion.35
  0.2 0.4 fusion.21
  0.6 0.7 subtract_convert_fusion
  1.4 4.0 %convolution_bitcast_fusion = f32[1024,256]{0,1:T(8,128)S(1)} fusion(bf16[1024,2400]{1,0:T(8,128)(2,1)} %bitcast.33, bf16[2400,128]{1,0:T(8,128)(2,1)S(1)} %bitcast.32, bf16[2400,128]{1,0:T(8,128)(2,1)S(1)} %bitcast.31), kind=kOutput, calls=%fused_computation | convolution fusion | flops 1260748800 | bytes 7192576 | tf_op jit(solution)/shard_map/dot_general | solution.py:38
  5.4 0.3 copy.6
  5.7 0.1 add_reduce_fusion
  5.8 0.1 fusion.8
  5.9 0.8 pad_maximum_fusion.1
  6.8 2.1 %collective-permute-start = (bf16[2,32,32,128]{3,2,1,0:T(8,128)(2,1)}, bf16[2,32,32,128]{3,2,1,0:T(8,128)(2,1)}, u32[]{:S(2)}, u32[]{:S(2)}) collective-permute-start(bf16[2,32,32,128]{3,2,1,0:T(8,128)(2,1)} %pad_maximum_fusion.1), channel_id=1, source_target_pairs={{0,1},{1,0},{2,3},{3,2},{4,5},{5,4},{6,7},{7,6},{8,9},{9,8},{10,11... | collective-permute-start | bytes 1572872 | tf_op jit(solution)/shard_map/ppermute | solution.py:196
  8.8 4.0 %convolution_bitcast_fusion.1 = f32[1024,256]{0,1:T(8,128)S(1)} fusion(bf16[1024,2400]{1,0:T(8,128)(2,1)} %bitcast.34, bf16[2400,128]{1,0:T(8,128)(2,1)S(1)} %bitcast.29, bf16[2400,128]{1,0:T(8,128)(2,1)S(1)} %bitcast.30), kind=kOutput, calls=%fused_computation.1 | convolution fusion | flops 1260748800 | bytes 7192576 | tf_op jit(solution)/shard_map/dot_general | solution.py:38
  12.9 0.3 copy.5
  13.2 0.1 add_reduce_fusion.1
  13.3 0.0 copy-done
  13.3 0.8 dynamic-slice_reduce_fusion.picks_ref
  14.1 0.1 fusion.6
  14.2 6.6 %collective-permute-done = bf16[2,32,32,128]{3,2,1,0:T(8,128)(2,1)} collective-permute-done((bf16[2,32,32,128]{3,2,1,0:T(8,128)(2,1)}, bf16[2,32,32,128]{3,2,1,0:T(8,128)(2,1)}, u32[]{:S(2)}, u32[]{:S(2)}) %collective-permute-start) | collective-permute-done | bytes 524320 | tf_op jit(solution)/shard_map/ppermute | solution.py:196
  20.8 1.2 broadcast_select_fusion.1
  22.0 0.1 maximum_bitcast_fusion
  22.1 0.1 copy.7
  22.2 1.7 %copy.9.x_ref.mine_ref = bf16[128,32,128]{2,1,0:T(8,128)(2,1)} copy(bf16[128,32,128]{0,2,1:T(8,128)(2,1)S(1)} %bitcast.28) | data formatting | bytes 2097152 | tf_op jit(solution)/shard_map/reshape | solution.py:203
  23.9 89.8 %shard_map.28.refs_0_.refs_1_.refs_2_ = bf16[16,128,32,128]{3,2,1,0:T(8,128)(2,1)} custom-call(bf16[128,32,128]{2,1,0:T(8,128)(2,1)} %copy.9.x_ref.mine_ref), custom_call_target="tpu_custom_call" | custom-call | tf_op jit(solution)/shard_map/pallas_call | solution.py:174
  113.8 10.6 %shard_map.29 = bf16[3,128,64,128]{3,2,1,0:T(8,128)(2,1)} custom-call(s32[3]{0:T(128)} %dynamic-slice_reduce_fusion.picks_ref, bf16[128,32,128]{2,1,0:T(8,128)(2,1)} %copy.9.x_ref.mine_ref, bf16[16,128,32,128]{3,2,1,0:T(8,128)(2,1)} %shard_map.28.refs_0_.refs_1_.refs_2_, bf16[16,128,32,128]{3,2,1,0:T(8,128)(2,1)} %shard_map.28.refs_0_.refs_1_.refs_2_, ...), custom_call_target="tpu_custom_call" | custom-call | tf_op jit(solution)/shard_map/pallas_call | solution.py:76
  (5 shorter events, 0.0 us)
Async XLA Ops:
  0.0 13.3 %copy-start = (s32[3,16]{1,0:T(4,128)S(1)}, s32[3,16]{1,0:T(4,128)}, u32[]{:S(2)}) copy-start(s32[3,16]{1,0:T(4,128)} %param.3) | copy-start | bytes 580
  6.8 14.0 %collective-permute-start = (bf16[2,32,32,128]{3,2,1,0:T(8,128)(2,1)}, bf16[2,32,32,128]{3,2,1,0:T(8,128)(2,1)}, u32[]{:S(2)}, u32[]{:S(2)}) collective-permute-start(bf16[2,32,32,128]{3,2,1,0:T(8,128)(2,1)} %pad_maximum_fusion.1), channel_id=1, source_target_pairs={{0,1},{1,0},{2,3},{3,2},{4,5},{5,4},{6,7},{7,6},{8,9},{9,8},{10,11... | collective-permute-start | bytes 1572872 | tf_op jit(solution)/shard_map/ppermute | solution.py:196
